TPU v7x, 32 devices: a whole 2x2x4 slice. The times are simulated.
32 devices in a mesh: outer: 4 (over z), inner: 8 (over y, x, core).
Axes of the slice: x: 2, y: 2, z: 4, core: 2. Of those that a mesh axis runs over, the one named last changes fastest.
Arguments:
- field_slab: float32 [512, 32, 1024], P(None, 'inner', 'outer'), may hold values from -48 to 48, as said below
- start_block: float32 [512, 256], replicated, may hold values from -6 to 6
Outputs:
- factor: float32 [512, 256], replicated
- core_fibres: float32 [256, 32, 1024], P('inner', None, 'outer')
Inputs may be any that keep to these rules, and one draw needn't show every extreme that they name: `field_slab`: real values.
All inputs are finite; a program needn't handle non-finite values.
Results may differ from a plain program's by a relative error of at most 0.00016.
Values sent between devices are 32-bit elements; how exact they have to be, the bound alone decides.
A program may use at most 64 MiB of HBM per device.

v0:
```python
import jax
import jax.numpy as jnp
from jax import lax
from jax.experimental import pallas as pl
from jax.experimental.pallas import tpu as pltpu
from jax.sharding import PartitionSpec as P

ITERS = 2
BLOCK = 16
LANES = 128
HIGHEST = lax.Precision.HIGHEST


def dot(a, b, dims, precision=HIGHEST):
    return lax.dot_general(
        a, b, ((dims[0], dims[1]), ((), ())), precision=precision,
        preferred_element_type=jnp.float32,
    )


def inverse_factor(mat, inv):
    n = mat.shape[0]
    rows = lax.broadcasted_iota(jnp.int32, (n, n), 0)
    cols = lax.broadcasted_iota(jnp.int32, (n, n), 1)
    inv[...] = jnp.where(rows == cols, 1.0, 0.0).astype(jnp.float32)
    sub = lax.broadcasted_iota(jnp.int32, (BLOCK, LANES), 0)
    for r0 in range(0, n, BLOCK):
        r1 = r0 + BLOCK
        left = (r0 // LANES) * LANES
        right = -(-r1 // LANES) * LANES
        tiles = [mat[r0:r1, c : c + LANES] for c in range(left, n, LANES)]
        split = len(tiles)
        tiles += [inv[r0:r1, c : c + LANES] for c in range(0, right, LANES)]
        at = r0 - left
        wide = [
            jnp.broadcast_to(tiles[0][:, at + k : at + k + 1], (BLOCK, LANES))
            for k in range(BLOCK)
        ]
        scale = jnp.zeros((BLOCK, LANES), jnp.float32)
        for j in range(BLOCK):
            root = lax.rsqrt(wide[j][j : j + 1, :])
            column = jnp.where(sub > j, wide[j] * (root * root), 0.0)
            scale = jnp.where(sub == j, root, scale)
            for k in range(j + 1, BLOCK):
                wide[k] = wide[k] - column * wide[k][j : j + 1, :]
            tiles = [t - column * t[j : j + 1, :] for t in tiles]
        tiles = [t * scale for t in tiles]
        for i, c in enumerate(range(0, right, LANES)):
            inv[r0:r1, c : c + LANES] = tiles[split + i]
        if r1 == n:
            break
        upper = jnp.concatenate(tiles[:split], axis=1) if split > 1 else tiles[0]
        lower = (
            jnp.concatenate(tiles[split:], axis=1) if len(tiles) - split > 1 else tiles[split]
        )
        both = jnp.concatenate([upper, lower], axis=1)
        for a0, a1 in ((r1, r1 + BLOCK), (r1 + BLOCK, n)):
            if a0 >= a1:
                continue
            step = dot(upper[:, a0 - left : a1 - left], both, ((0,), (0,)))
            mat[a0:a1, left:n] = mat[a0:a1, left:n] - step[:, : n - left]
            inv[a0:a1, 0:right] = inv[a0:a1, 0:right] - step[:, n - left :]


def orthonormal(block_t, mat, inv):
    mat[...] = dot(block_t, block_t, ((1,), (1,)))
    inverse_factor(mat, inv)
    return dot(inv[...], block_t, ((1,), (0,)))


def start_kernel(start_ref, basis_ref, mat, inv):
    basis_ref[...] = orthonormal(start_ref[...].T, mat, inv)


def sweeps_kernel(gram_ref, basis_ref, out_ref, factor_ref, mat, inv):
    out_ref[...] = basis_ref[...]

    def sweep(_, carry):
        out_ref[...] = orthonormal(
            dot(out_ref[...], gram_ref[...], ((1,), (0,))), mat, inv
        )
        return carry

    lax.fori_loop(0, ITERS, sweep, 0)
    factor_ref[...] = out_ref[...].T


def call(kernel, outs, rank, *args):
    return pl.pallas_call(
        kernel,
        out_shape=[jax.ShapeDtypeStruct(s, jnp.float32) for s in outs],
        in_specs=[pl.BlockSpec(memory_space=pltpu.VMEM)] * len(args),
        out_specs=[pl.BlockSpec(memory_space=pltpu.VMEM)] * len(outs),
        scratch_shapes=[pltpu.VMEM((rank, rank), jnp.float32)] * 2,
        compiler_params=pltpu.CompilerParams(vmem_limit_bytes=32 * 2**20),
        cost_estimate=pl.CostEstimate(
            flops=2 * 10**9, bytes_accessed=4 * 2**20, transcendentals=0
        ),
    )(*args)


def on_device(field_slab, start_block):
    order, second, third = field_slab.shape
    rank = start_block.shape[1]
    unfolded = field_slab.reshape(order, second * third)
    gram_local = dot(unfolded, unfolded, ((1,), (1,)))
    (basis,) = call(start_kernel, [(rank, order)], rank, start_block)
    gram_total = lax.psum(gram_local, ("outer", "inner"))
    basis, factor = call(
        sweeps_kernel, [(rank, order), (order, rank)], rank, gram_total, basis
    )
    core = dot(basis, unfolded, ((1,), (0,))).reshape(rank, second, third)
    core = lax.all_to_all(core, "inner", split_axis=0, concat_axis=1, tiled=True)
    return (factor, core)


def solution(mesh):
    return jax.shard_map(
        on_device,
        mesh=mesh,
        in_specs=(P(None, "inner", "outer"), P()),
        out_specs=(P(), P("inner", None, "outer")),
        check_vma=False,
    )
```

profile of v0, /device:TPU:0, one launch (start us, length us, event | category | flops | bytes accessed | tf_op | source)
XLA Modules:
  0.0 203.2 jit_solution(13838847348772212664)
XLA Ops:
  7.2 0.0 copy-start.2
  7.2 0.0 all-reduce.2.cloned.1.call-start
  7.2 7.2 %fusion.2 = f32[512,512]{1,0:T(8,128)} fusion(f32[512,4,256]{2,1,0:T(4,128)} %param.2), kind=kOutput, calls=%fused_computation.2 | convolution fusion | flops 3221225472 | bytes 3145728 | tf_op jit(solution)/shard_map/dot_general | solution.py:15
  14.5 0.0 all-reduce.2.cloned.1.call-update
  14.5 0.0 copy-done.2
  14.5 1.8 copy.13
  16.3 0.0 copy-start.1
  16.3 2.0 copy.10
  18.3 0.0 copy-done.1
  18.3 11.0 %shard_map.41.basis_ref = f32[256,512]{1,0:T(8,128)S(1)} custom-call(f32[512,256]{1,0:T(8,128)S(1)} %copy-done.1), custom_call_target="tpu_custom_call" | custom-call | flops 2000000000 | bytes 4194304 | tf_op jit(solution)/shard_map/pallas_call | solution.py:89
  29.3 117.9 %all-reduce.2.cloned.1.call-done.gram_ref = f32[512,512]{1,0:T(8,128)} async-done(((f32[512,512]{1,0:T(8,128)}), f32[512,512]{1,0:T(8,128)}) %all-reduce.2.cloned.1.call-update) | async-done | bytes 1048592 | tf_op jit(solution)/shard_map/psum | solution.py:108
  147.2 0.0 copy-start
  147.2 1.2 copy-done
  148.4 25.0 %shard_map.42 = (f32[256,512]{1,0:T(8,128)S(1)}, f32[512,256]{1,0:T(8,128)}) custom-call(f32[512,512]{1,0:T(8,128)S(1)} %copy-done, f32[256,512]{1,0:T(8,128)S(1)} %shard_map.41.basis_ref), custom_call_target="tpu_custom_call" | custom-call | flops 2000000000 | bytes 4194304 | tf_op jit(solution)/shard_map/pallas_call | solution.py:89
  173.4 1.9 fusion.5
  175.3 0.7 copy.11
  176.0 18.7 %all_to_all.18 = f32[256,4,256]{2,1,0:T(4,128)S(1)} all-to-all(f32[256,4,256]{2,1,0:T(4,128)S(1)} %copy.11), channel_id=1, replica_groups=mesh['outer'=4,'inner'=8] {'inner'}, dimensions={0} | all-to-all | bytes 2097152 | tf_op jit(solution)/shard_map/all_to_all | solution.py:113
  194.8 0.3 copy.12
  195.0 1.3 all_to_all.16
Async XLA Ops:
  7.2 7.3 %copy-start.2 = (f32[512,4,256]{2,1,0:T(4,128)S(1)}, f32[512,4,256]{2,1,0:T(4,128)}, u32[]{:S(2)}) copy-start(f32[512,4,256]{2,1,0:T(4,128)} %param.2) | copy-start | bytes 6291460
  7.2 140.0 %all-reduce.2.cloned.1.call-start = ((), (), s32[]{:S(2)}) async-start(), calls=%async_computation.1 | async-start | bytes 2097152 | tf_op jit(solution)/shard_map/psum | solution.py:108
  16.3 2.0 copy-start.1
  147.2 1.2 copy-start
Sparse Core Ops, SparseCore 0:
  14.6 132.5 all-reduce.1
where the time goes:
time: 203 us
  waiting for transfers between devices  118 us (58%)
  Pallas kernels  36 us (18%)
  blocking collectives  18.7 us (9%)
  between operations  14.1 us (7%)
  matrix products  9.16 us (5%)
  local copies, waits for them, and re-layouts  7.3 us (4%)
    psum x1, waiting for transfers between devices, on_device(): gram_total = lax.psum(gram_local, ('outer', 'inner'))  118 us
    pallas_call x2, Pallas kernels, call(): pl.pallas_call(kernel, out_shape=[jax.ShapeDtypeStruct(s, jnp.float32) fo...  36 us
    all_to_all x1, blocking collectives, on_device(): lax.all_to_all(core, 'inner', split_axis=0, concat_axis=1, tiled=True)  18.7 us
    dot_general x2, matrix products, dot(): lax.dot_general(a, b, ((dims[0], dims[1]), ((), ())), precision=precision...  9.16 us
  transfers between devices with their start and end apart: 1, of which 1 were waited for; matrix products, arithmetic and copies ran while one was open for 2% of the time, Pallas kernels for 5%

commit v1 on v0

--- a/solution.py
+++ b/solution.py
@@ -1,3 +1,5 @@
+import functools
+
 import jax
 import jax.numpy as jnp
 from jax import lax
@@ -9,6 +11,7 @@
 BLOCK = 16
 LANES = 128
 HIGHEST = lax.Precision.HIGHEST
+HIGH = lax.Precision.HIGH
 
 
 def dot(a, b, dims, precision=HIGHEST):
@@ -99,24 +102,271 @@
     )(*args)
 
 
-def on_device(field_slab, start_block):
+MESH = pl.DeviceIdType.MESH
+
+
+def upper_blocks(order):
+    count = order // LANES
+    return [(i, j) for i in range(count) for j in range(i, count)]
+
+
+def peers(n_out, n_in):
+    out, inn = lax.axis_index("outer"), lax.axis_index("inner")
+    core, chip, chips = lax.rem(inn, 2), inn // 2, n_in // 2
+    twin = (out, inn + 1 - 2 * core)
+    plane = [
+        (lax.rem(chip + d, chips), lax.rem(chip + chips - d, chips)) for d in range(1, chips)
+    ]
+    line = [(lax.rem(out + d, n_out), lax.rem(out + n_out - d, n_out)) for d in range(1, n_out)]
+    return out, core, chip, twin, plane, line
+
+
+def rows_at(start, size):
+    return pl.ds(pl.multiple_of(start, 8), size)
+
+
+def remote(src, dst, sems, at, device):
+    return pltpu.make_async_remote_copy(
+        src_ref=src, dst_ref=dst, send_sem=sems[0].at[at], recv_sem=sems[1].at[at],
+        device_id=device, device_id_type=MESH,
+    )
+
+
+def gram_kernel(
+    n_out, n_in, field_ref, gram_ref, unfolded, part, total, got_core, got_chip, got_out,
+    load_sem, send_sem, recv_sem,
+):
+    order, second, third = field_ref.shape
+    out, core, chip, twin, plane, line = peers(n_out, n_in)
+    chips = n_in // 2
+    sems = (send_sem, recv_sem)
+    loads = [
+        pltpu.make_async_copy(
+            field_ref.at[:, i, :], unfolded.at[:, pl.ds(i * third, third)], load_sem.at[i]
+        )
+        for i in range(second)
+    ]
+    for load in loads:
+        load.start()
+    barrier = pltpu.get_barrier_semaphore()
+    pl.semaphore_signal(barrier, inc=1, device_id=twin, device_id_type=MESH)
+    for to, _ in plane:
+        pl.semaphore_signal(barrier, inc=1, device_id=(out, to * 2 + core), device_id_type=MESH)
+    for to, _ in line:
+        pl.semaphore_signal(
+            barrier, inc=1, device_id=(to, chip * 2 + core), device_id_type=MESH
+        )
+    for load in loads:
+        load.wait()
+
+    places = {pair: at for at, pair in enumerate(upper_blocks(order))}
+    size = len(places) * LANES
+    if part.shape[0] > size:
+        part[size:, :] = jnp.zeros((part.shape[0] - size, LANES), jnp.float32)
+    wide = 2 * LANES
+    for i in range(0, order, wide):
+        for j in range(i, order, wide):
+            block = dot(
+                unfolded[i : i + wide, :], unfolded[j : j + wide, :], ((1,), (1,)), HIGH
+            )
+            for a in range(2):
+                for b in range(2):
+                    pair = (i // LANES + a, j // LANES + b)
+                    if pair in places:
+                        at = places[pair] * LANES
+                        part[at : at + LANES, :] = block[
+                            a * LANES : (a + 1) * LANES, b * LANES : (b + 1) * LANES
+                        ]
+
+    pl.semaphore_wait(barrier, 1 + len(plane) + len(line))
+
+    half = part.shape[0] // 2
+    quarter = half // chips
+    piece = quarter // n_out
+    mine = core * half
+    copy = remote(part.at[rows_at((1 - core) * half, half)], got_core, sems, 0, twin)
+    copy.start()
+    copy.wait()
+    part[rows_at(mine, half), :] += got_core[...]
+
+    copies = []
+    for d, (to, _) in enumerate(plane):
+        copies.append(
+            remote(
+                part.at[rows_at(mine + to * quarter, quarter)], got_chip.at[d], sems, 1 + d,
+                (out, to * 2 + core),
+            )
+        )
+        copies[-1].start()
+    for copy in copies:
+        copy.wait()
+    mine = mine + chip * quarter
+    value = part[rows_at(mine, quarter), :]
+    for d in range(len(plane)):
+        value += got_chip[d]
+    part[rows_at(mine, quarter), :] = value
+
+    base = 1 + len(plane)
+    copies = []
+    for d, (to, _) in enumerate(line):
+        copies.append(
+            remote(
+                part.at[rows_at(mine + to * piece, piece)], got_out.at[d], sems, base + d,
+                (to, chip * 2 + core),
+            )
+        )
+        copies[-1].start()
+    for copy in copies:
+        copy.wait()
+    own = mine + out * piece
+    value = part[rows_at(own, piece), :]
+    for d in range(len(line)):
+        value += got_out[d]
+    total[rows_at(own, piece), :] = value
+
+    base += len(line)
+    copies = []
+    for d, (to, _) in enumerate(line):
+        spot = total.at[rows_at(own, piece)]
+        copies.append(remote(spot, spot, sems, base + d, (to, chip * 2 + core)))
+        copies[-1].start()
+    for copy in copies:
+        copy.wait()
+    base += len(line)
+    copies = []
+    for d, (to, _) in enumerate(plane):
+        spot = total.at[rows_at(mine, quarter)]
+        copies.append(remote(spot, spot, sems, base + d, (out, to * 2 + core)))
+        copies[-1].start()
+    for copy in copies:
+        copy.wait()
+    base += len(plane)
+    spot = total.at[rows_at(core * half, half)]
+    copy = remote(spot, spot, sems, base, twin)
+    copy.start()
+    copy.wait()
+
+    for (i, j), at in places.items():
+        block = total[at * LANES : (at + 1) * LANES, :]
+        gram_ref[i * LANES : (i + 1) * LANES, j * LANES : (j + 1) * LANES] = block
+        if i != j:
+            gram_ref[j * LANES : (j + 1) * LANES, i * LANES : (i + 1) * LANES] = block.T
+
+
+def gram_sum(mesh, field_slab):
+    n_out, n_in = mesh.shape["outer"], mesh.shape["inner"]
     order, second, third = field_slab.shape
+    chips = n_in // 2
+    unit = 8 * n_out * n_in
+    rows = -(-len(upper_blocks(order)) * LANES // unit) * unit
+    half = rows // 2
+    sems = 2 + 2 * (chips - 1) + 2 * (n_out - 1)
+    f32 = jnp.float32
+    return pl.pallas_call(
+        functools.partial(gram_kernel, n_out, n_in),
+        out_shape=jax.ShapeDtypeStruct((order, order), f32),
+        in_specs=[pl.BlockSpec(memory_space=pl.ANY)],
+        out_specs=pl.BlockSpec(memory_space=pltpu.VMEM),
+        scratch_shapes=[
+            pltpu.VMEM((order, second * third), f32),
+            pltpu.VMEM((rows, LANES), f32),
+            pltpu.VMEM((rows, LANES), f32),
+            pltpu.VMEM((half, LANES), f32),
+            pltpu.VMEM((max(chips - 1, 1), half // chips, LANES), f32),
+            pltpu.VMEM((max(n_out - 1, 1), half // chips // n_out, LANES), f32),
+            pltpu.SemaphoreType.DMA((second,)),
+            pltpu.SemaphoreType.DMA((sems,)),
+            pltpu.SemaphoreType.DMA((sems,)),
+        ],
+        compiler_params=pltpu.CompilerParams(
+            collective_id=0, has_side_effects=True, vmem_limit_bytes=40 * 2**20
+        ),
+    )(field_slab)
+
+
+def core_kernel(n_in, basis_ref, field_ref, fibres_ref, unfolded, core, load_sem, send_sem, recv_sem):
+    order, second, third = field_ref.shape
+    rank = basis_ref.shape[0]
+    share = rank // n_in
+    out, inn = lax.axis_index("outer"), lax.axis_index("inner")
+    loads = [
+        pltpu.make_async_copy(field_ref.at[:, i, :], unfolded.at[i], load_sem.at[i])
+        for i in range(second)
+    ]
+    for load in loads:
+        load.start()
+    barrier = pltpu.get_barrier_semaphore()
+    targets = [lax.rem(inn + d, n_in) for d in range(1, n_in)]
+    for to in targets:
+        pl.semaphore_signal(barrier, inc=1, device_id=(out, to), device_id_type=MESH)
+    copies = []
+    for i in range(second):
+        loads[i].wait()
+        core[i] = dot(basis_ref[...], unfolded[i], ((1,), (0,)), HIGH)
+        if i == 0:
+            pl.semaphore_wait(barrier, n_in - 1)
+        for d, to in enumerate(targets):
+            copies.append(
+                pltpu.make_async_remote_copy(
+                    src_ref=core.at[i, rows_at(to * share, share)],
+                    dst_ref=fibres_ref.at[inn * second + i],
+                    send_sem=send_sem.at[i, d],
+                    recv_sem=recv_sem.at[i, d],
+                    device_id=(out, to),
+                    device_id_type=MESH,
+                )
+            )
+            copies[-1].start()
+        copies.append(
+            pltpu.make_async_copy(
+                core.at[i, rows_at(inn * share, share)],
+                fibres_ref.at[inn * second + i],
+                load_sem.at[second + i],
+            )
+        )
+        copies[-1].start()
+    for copy in copies:
+        copy.wait()
+
+
+def core_exchange(mesh, basis, field_slab):
+    n_in = mesh.shape["inner"]
+    order, second, third = field_slab.shape
+    rank = basis.shape[0]
+    f32 = jnp.float32
+    return pl.pallas_call(
+        functools.partial(core_kernel, n_in),
+        out_shape=jax.ShapeDtypeStruct((n_in * second, rank // n_in, third), f32),
+        in_specs=[pl.BlockSpec(memory_space=pltpu.VMEM), pl.BlockSpec(memory_space=pl.ANY)],
+        out_specs=pl.BlockSpec(memory_space=pl.ANY),
+        scratch_shapes=[
+            pltpu.VMEM((second, order, third), f32),
+            pltpu.VMEM((second, rank, third), f32),
+            pltpu.SemaphoreType.DMA((2 * second,)),
+            pltpu.SemaphoreType.DMA((second, n_in - 1)),
+            pltpu.SemaphoreType.DMA((second, n_in - 1)),
+        ],
+        compiler_params=pltpu.CompilerParams(
+            collective_id=1, has_side_effects=True, vmem_limit_bytes=40 * 2**20
+        ),
+    )(basis, field_slab)
+
+
+def on_device(mesh, field_slab, start_block):
+    order = field_slab.shape[0]
     rank = start_block.shape[1]
-    unfolded = field_slab.reshape(order, second * third)
-    gram_local = dot(unfolded, unfolded, ((1,), (1,)))
     (basis,) = call(start_kernel, [(rank, order)], rank, start_block)
-    gram_total = lax.psum(gram_local, ("outer", "inner"))
+    gram_total = gram_sum(mesh, field_slab)
     basis, factor = call(
         sweeps_kernel, [(rank, order), (order, rank)], rank, gram_total, basis
     )
-    core = dot(basis, unfolded, ((1,), (0,))).reshape(rank, second, third)
-    core = lax.all_to_all(core, "inner", split_axis=0, concat_axis=1, tiled=True)
-    return (factor, core)
+    fibres = core_exchange(mesh, basis, field_slab)
+    return (factor, fibres.transpose(1, 0, 2))
 
 
 def solution(mesh):
     return jax.shard_map(
-        on_device,
+        functools.partial(on_device, mesh),
         mesh=mesh,
         in_specs=(P(None, "inner", "outer"), P()),
         out_specs=(P(), P("inner", None, "outer")),

time: 203 us -> 84.7 us (0.42)
  waiting for transfers between devices: 118 us -> 0 us
  Pallas kernels: 36 us -> 81.1 us
  blocking collectives: 18.7 us -> 0 us
  between operations: 14.1 us -> 0.68 us
  matrix products: 9.16 us -> 0 us
  local copies, waits for them, and re-layouts: 7.3 us -> 2.77 us
    psum x1 -> x0, waiting for transfers between devices: 118 us -> none  [on_device(): gram_total = lax.psum(gram_local, ('outer', 'inner'))]
    pallas_call x0 -> x2, Pallas kernels: none -> 45 us  [the longest x1 28.4 us: gram_sum(): pl.pallas_call(functools.partial(gram_kernel, n_out, n_in), out_shape=jax...]
    all_to_all x1 -> x0, blocking collectives: 18.7 us -> none  [on_device(): lax.all_to_all(core, 'inner', split_axis=0, concat_axis=1, tiled=True)]
    dot_general x2 -> x0, matrix products: 9.16 us -> none  [dot(): lax.dot_general(a, b, ((dims[0], dims[1]), ((), ())), precision=precision...]
    dot_general x2 -> x0, local copies, waits for them, and re-layouts: 2.66 us -> none  [dot(): lax.dot_general(a, b, ((dims[0], dims[1]), ((), ())), precision=precision...]
  transfers between devices with their start and end apart: 1 -> 0, of which waited for: 1 -> 0; matrix products, arithmetic and copies ran while one was open for 2% -> 0% of each run, Pallas kernels for 5% -> 0%
where the time goes in v1:
time: 84.7 us; the launch traced here: 84.5 us
  Pallas kernels  81.1 us (96%)
  local copies, waits for them, and re-layouts  2.77 us (3%)
    pallas_call x2, Pallas kernels, call(): pl.pallas_call(kernel, out_shape=[jax.ShapeDtypeStruct(s, jnp.float32) fo...  36 us
    pallas_call x1, Pallas kernels, gram_sum(): pl.pallas_call(functools.partial(gram_kernel, n_out, n_in), out_shape=jax...  28.4 us
    pallas_call x1, Pallas kernels, core_exchange(): pl.pallas_call(functools.partial(core_kernel, n_in), out_shape=jax.ShapeD...  16.7 us
    unnamed x5, local copies, waits for them, and re-layouts  2.77 us

profile of v1, /device:TPU:0, one launch (start us, length us, event | category | flops | bytes accessed | tf_op | source)
XLA Modules:
  0.0 84.5 jit_solution(1910667994083725609)
XLA Ops:
  0.6 0.0 copy-start
  0.6 0.0 copy-start.1
  0.6 1.2 %copy-done.1 = f32[512,256]{1,0:T(8,128)S(1)} copy-done((f32[512,256]{1,0:T(8,128)S(1)}, f32[512,256]{1,0:T(8,128)}, u32[]{:S(2)}) %copy-start.1) | copy-done | bytes 524312
  1.8 11.0 %shard_map.42.basis_ref = f32[256,512]{1,0:T(8,128)S(1)} custom-call(f32[512,256]{1,0:T(8,128)S(1)} %copy-done.1), custom_call_target="tpu_custom_call" | custom-call | flops 2000000000 | bytes 4194304 | tf_op jit(solution)/shard_map/pallas_call | solution.py:92
  12.8 0.0 copy-done
  12.8 28.4 %shard_map.41.gram_ref = f32[512,512]{1,0:T(8,128)S(1)} custom-call(f32[512,4,256]{2,1,0:T(4,128)S(1)} %copy-done), custom_call_target="tpu_custom_call" | custom-call | tf_op jit(solution)/shard_map/pallas_call | solution.py:265
  41.2 25.0 %shard_map.43 = (f32[256,512]{1,0:T(8,128)S(1)}, f32[512,256]{1,0:T(8,128)}) custom-call(f32[512,512]{1,0:T(8,128)S(1)} %shard_map.41.gram_ref, f32[256,512]{1,0:T(8,128)S(1)} %shard_map.42.basis_ref), custom_call_target="tpu_custom_call" | custom-call | flops 2000000000 | bytes 4194304 | tf_op jit(solution)/shard_map/pallas_call | solution.py:92
  66.3 16.7 %shard_map.44 = f32[32,32,256]{2,1,0:T(8,128)S(1)} custom-call(f32[256,512]{1,0:T(8,128)S(1)} %get-tuple-element.5.basis_ref, f32[512,4,256]{2,1,0:T(4,128)S(1)} %copy-done), custom_call_target="tpu_custom_call" | custom-call | tf_op jit(solution)/shard_map/pallas_call | solution.py:337
  82.9 1.6 %copy.4 = f32[32,32,256]{2,1,0:T(8,128)} copy(f32[32,32,256]{2,0,1:T(8,128)S(1)} %bitcast.1) | data formatting | bytes 2097152
Async XLA Ops:
  0.6 12.2 %copy-start = (f32[512,4,256]{2,1,0:T(4,128)S(1)}, f32[512,4,256]{2,1,0:T(4,128)}, u32[]{:S(2)}) copy-start(f32[512,4,256]{2,1,0:T(4,128)} %field_ref.3) | copy-start | bytes 6291460
  0.6 1.2 %copy-start.1 = (f32[512,256]{1,0:T(8,128)S(1)}, f32[512,256]{1,0:T(8,128)}, u32[]{:S(2)}) copy-start(f32[512,256]{1,0:T(8,128)} %start_ref.1) | copy-start | bytes 1572868

commit v2 on v1

--- a/solution.py
+++ b/solution.py
@@ -9,6 +9,7 @@
 
 ITERS = 2
 BLOCK = 16
+SUB = 8
 LANES = 128
 HIGHEST = lax.Precision.HIGHEST
 HIGH = lax.Precision.HIGH
@@ -21,58 +22,99 @@
     )
 
 
+def eliminate(wide, tiles):
+    sub = lax.broadcasted_iota(jnp.int32, (SUB, LANES), 0)
+    pieces = BLOCK // SUB
+
+    def row(x, i):
+        return jnp.broadcast_to(x[i : i + 1, :], (SUB, LANES))
+
+    for s in range(pieces):
+        at = s * SUB
+        splat = [[row(wide[at + k][s], i) for i in range(k, SUB)] for k in range(SUB)]
+        root, low = [], []
+        for j in range(SUB):
+            root.append(lax.rsqrt(splat[j][0]))
+            low.append([x * root[j] for x in splat[j][1:]])
+            for k in range(j + 1, SUB):
+                by = low[j][k - j - 1]
+                splat[k] = [
+                    x - low[j][k - j - 1 + i] * by for i, x in enumerate(splat[k])
+                ]
+        columns, scale = [], jnp.zeros((SUB, LANES), jnp.float32)
+        for j in range(SUB):
+            column = jnp.zeros((SUB, LANES), jnp.float32)
+            for i in range(j + 1, SUB):
+                column = jnp.where(sub == i, low[j][i - j - 1], column)
+            columns.append({s: column})
+            scale = jnp.where(sub == j, root[j], scale)
+        for h in range(s + 1, pieces):
+            for j in range(SUB):
+                columns[j][h] = wide[at + j][h] * root[j]
+                for k in range(j + 1, SUB):
+                    wide[at + k][h] = wide[at + k][h] - columns[j][h] * low[j][k - j - 1]
+        for t in range(s + 1, pieces):
+            for k in range(SUB):
+                for j in range(SUB):
+                    by = row(columns[j][t], k)
+                    for h in range(t, pieces):
+                        spot = t * SUB + k
+                        wide[spot][h] = wide[spot][h] - columns[j][h] * by
+        for tile in tiles:
+            for j in range(SUB):
+                by = row(tile[s], j) * root[j]
+                for h in range(s, pieces):
+                    if h > s or j < SUB - 1:
+                        tile[h] = tile[h] - columns[j][h] * by
+            tile[s] = tile[s] * scale
+
+
 def inverse_factor(mat, inv):
     n = mat.shape[0]
     rows = lax.broadcasted_iota(jnp.int32, (n, n), 0)
     cols = lax.broadcasted_iota(jnp.int32, (n, n), 1)
     inv[...] = jnp.where(rows == cols, 1.0, 0.0).astype(jnp.float32)
-    sub = lax.broadcasted_iota(jnp.int32, (BLOCK, LANES), 0)
     for r0 in range(0, n, BLOCK):
         r1 = r0 + BLOCK
         left = (r0 // LANES) * LANES
         right = -(-r1 // LANES) * LANES
-        tiles = [mat[r0:r1, c : c + LANES] for c in range(left, n, LANES)]
+        pieces = range(r0, r1, SUB)
+        tiles = [
+            [mat[r : r + SUB, c : c + LANES] for r in pieces] for c in range(left, n, LANES)
+        ]
         split = len(tiles)
-        tiles += [inv[r0:r1, c : c + LANES] for c in range(0, right, LANES)]
+        tiles += [
+            [inv[r : r + SUB, c : c + LANES] for r in pieces] for c in range(0, right, LANES)
+        ]
         at = r0 - left
         wide = [
-            jnp.broadcast_to(tiles[0][:, at + k : at + k + 1], (BLOCK, LANES))
+            {
+                h: jnp.broadcast_to(tiles[0][h][:, at + k : at + k + 1], (SUB, LANES))
+                for h in range(k // SUB, BLOCK // SUB)
+            }
             for k in range(BLOCK)
         ]
-        scale = jnp.zeros((BLOCK, LANES), jnp.float32)
-        for j in range(BLOCK):
-            root = lax.rsqrt(wide[j][j : j + 1, :])
-            column = jnp.where(sub > j, wide[j] * (root * root), 0.0)
-            scale = jnp.where(sub == j, root, scale)
-            for k in range(j + 1, BLOCK):
-                wide[k] = wide[k] - column * wide[k][j : j + 1, :]
-            tiles = [t - column * t[j : j + 1, :] for t in tiles]
-        tiles = [t * scale for t in tiles]
+        eliminate(wide, tiles)
         for i, c in enumerate(range(0, right, LANES)):
-            inv[r0:r1, c : c + LANES] = tiles[split + i]
-        if r1 == n:
-            break
-        upper = jnp.concatenate(tiles[:split], axis=1) if split > 1 else tiles[0]
-        lower = (
-            jnp.concatenate(tiles[split:], axis=1) if len(tiles) - split > 1 else tiles[split]
-        )
-        both = jnp.concatenate([upper, lower], axis=1)
-        for a0, a1 in ((r1, r1 + BLOCK), (r1 + BLOCK, n)):
-            if a0 >= a1:
-                continue
-            step = dot(upper[:, a0 - left : a1 - left], both, ((0,), (0,)))
-            mat[a0:a1, left:n] = mat[a0:a1, left:n] - step[:, : n - left]
-            inv[a0:a1, 0:right] = inv[a0:a1, 0:right] - step[:, n - left :]
+            for h, r in enumerate(pieces):
+                inv[r : r + SUB, c : c + LANES] = tiles[split + i][h]
+        if r1 < n:
+            full = [jnp.concatenate(t, axis=0) for t in tiles]
+            upper = jnp.concatenate(full[:split], axis=1) if split > 1 else full[0]
+            both = jnp.concatenate(full, axis=1)
+            for a0, a1 in ((r1, r1 + BLOCK), (r1 + BLOCK, n)):
+                if a0 < a1:
+                    step = dot(upper[:, a0 - left : a1 - left], both, ((0,), (0,)))
+                    mat[a0:a1, left:n] = mat[a0:a1, left:n] - step[:, : n - left]
+                    inv[a0:a1, 0:right] = inv[a0:a1, 0:right] - step[:, n - left :]
+        yield
 
 
 def orthonormal(block_t, mat, inv):
     mat[...] = dot(block_t, block_t, ((1,), (1,)))
-    inverse_factor(mat, inv)
+    for _ in inverse_factor(mat, inv):
+        pass
     return dot(inv[...], block_t, ((1,), (0,)))
-
-
-def start_kernel(start_ref, basis_ref, mat, inv):
-    basis_ref[...] = orthonormal(start_ref[...].T, mat, inv)
 
 
 def sweeps_kernel(gram_ref, basis_ref, out_ref, factor_ref, mat, inv):
@@ -133,8 +175,8 @@
 
 
 def gram_kernel(
-    n_out, n_in, field_ref, gram_ref, unfolded, part, total, got_core, got_chip, got_out,
-    load_sem, send_sem, recv_sem,
+    n_out, n_in, field_ref, start_ref, gram_ref, basis_ref, unfolded, part, total, got_core, got_chip, got_out, mat,
+    inv, load_sem, send_sem, recv_sem,
 ):
     order, second, third = field_ref.shape
     out, core, chip, twin, plane, line = peers(n_out, n_in)
@@ -178,6 +220,15 @@
                             a * LANES : (a + 1) * LANES, b * LANES : (b + 1) * LANES
                         ]
 
+    start = start_ref[...]
+    mat[...] = dot(start, start, ((0,), (0,)))
+    blocks = inverse_factor(mat, inv)
+    count = mat.shape[0] // BLOCK
+
+    def run(steps):
+        for _ in range(steps):
+            next(blocks, None)
+
     pl.semaphore_wait(barrier, 1 + len(plane) + len(line))
 
     half = part.shape[0] // 2
@@ -186,6 +237,7 @@
     mine = core * half
     copy = remote(part.at[rows_at((1 - core) * half, half)], got_core, sems, 0, twin)
     copy.start()
+    run(2)
     copy.wait()
     part[rows_at(mine, half), :] += got_core[...]
 
@@ -198,6 +250,7 @@
             )
         )
         copies[-1].start()
+    run(5)
     for copy in copies:
         copy.wait()
     mine = mine + chip * quarter
@@ -216,6 +269,7 @@
             )
         )
         copies[-1].start()
+    run(3)
     for copy in copies:
         copy.wait()
     own = mine + out * piece
@@ -230,6 +284,7 @@
         spot = total.at[rows_at(own, piece)]
         copies.append(remote(spot, spot, sems, base + d, (to, chip * 2 + core)))
         copies[-1].start()
+    run(3)
     for copy in copies:
         copy.wait()
     base += len(line)
@@ -238,12 +293,14 @@
         spot = total.at[rows_at(mine, quarter)]
         copies.append(remote(spot, spot, sems, base + d, (out, to * 2 + core)))
         copies[-1].start()
+    run(count)
     for copy in copies:
         copy.wait()
     base += len(plane)
     spot = total.at[rows_at(core * half, half)]
     copy = remote(spot, spot, sems, base, twin)
     copy.start()
+    basis_ref[...] = dot(inv[...], start_ref[...], ((1,), (1,)))
     copy.wait()
 
     for (i, j), at in places.items():
@@ -253,7 +310,8 @@
             gram_ref[j * LANES : (j + 1) * LANES, i * LANES : (i + 1) * LANES] = block.T
 
 
-def gram_sum(mesh, field_slab):
+def gram_sum(mesh, field_slab, start_block):
+    rank = start_block.shape[1]
     n_out, n_in = mesh.shape["outer"], mesh.shape["inner"]
     order, second, third = field_slab.shape
     chips = n_in // 2
@@ -264,9 +322,12 @@
     f32 = jnp.float32
     return pl.pallas_call(
         functools.partial(gram_kernel, n_out, n_in),
-        out_shape=jax.ShapeDtypeStruct((order, order), f32),
-        in_specs=[pl.BlockSpec(memory_space=pl.ANY)],
-        out_specs=pl.BlockSpec(memory_space=pltpu.VMEM),
+        out_shape=[
+            jax.ShapeDtypeStruct((order, order), f32),
+            jax.ShapeDtypeStruct((rank, order), f32),
+        ],
+        in_specs=[pl.BlockSpec(memory_space=pl.ANY), pl.BlockSpec(memory_space=pltpu.VMEM)],
+        out_specs=[pl.BlockSpec(memory_space=pltpu.VMEM)] * 2,
         scratch_shapes=[
             pltpu.VMEM((order, second * third), f32),
             pltpu.VMEM((rows, LANES), f32),
@@ -274,6 +335,8 @@
             pltpu.VMEM((half, LANES), f32),
             pltpu.VMEM((max(chips - 1, 1), half // chips, LANES), f32),
             pltpu.VMEM((max(n_out - 1, 1), half // chips // n_out, LANES), f32),
+            pltpu.VMEM((rank, rank), f32),
+            pltpu.VMEM((rank, rank), f32),
             pltpu.SemaphoreType.DMA((second,)),
             pltpu.SemaphoreType.DMA((sems,)),
             pltpu.SemaphoreType.DMA((sems,)),
@@ -281,7 +344,7 @@
         compiler_params=pltpu.CompilerParams(
             collective_id=0, has_side_effects=True, vmem_limit_bytes=40 * 2**20
         ),
-    )(field_slab)
+    )(field_slab, start_block)
 
 
 def core_kernel(n_in, basis_ref, field_ref, fibres_ref, unfolded, core, load_sem, send_sem, recv_sem):
@@ -355,8 +418,7 @@
 def on_device(mesh, field_slab, start_block):
     order = field_slab.shape[0]
     rank = start_block.shape[1]
-    (basis,) = call(start_kernel, [(rank, order)], rank, start_block)
-    gram_total = gram_sum(mesh, field_slab)
+    gram_total, basis = gram_sum(mesh, field_slab, start_block)
     basis, factor = call(
         sweeps_kernel, [(rank, order), (order, rank)], rank, gram_total, basis
     )

time: 84.7 us -> 84.3 us (level)
  Pallas kernels: 81.1 us -> 79.2 us
  local copies, waits for them, and re-layouts: 2.77 us -> 4.21 us
    pallas_call x2 -> x1, Pallas kernels: 36 us -> 24.7 us  [call(): pl.pallas_call(kernel, out_shape=[jax.ShapeDtypeStruct(s, jnp.float32) fo...]
    pallas_call x1, Pallas kernels: 28.4 us -> 37.9 us  [gram_sum(): pl.pallas_call(functools.partial(gram_kernel, n_out, n_in), out_shape=[ja...]
    unnamed x5, local copies, waits for them, and re-layouts: 2.77 us -> 4.21 us
where the time goes in v2:
time: 84.3 us; the launch traced here: 84.1 us
  Pallas kernels  79.2 us (94%)
  local copies, waits for them, and re-layouts  4.21 us (5%)
    pallas_call x1, Pallas kernels, gram_sum(): pl.pallas_call(functools.partial(gram_kernel, n_out, n_in), out_shape=[ja...  37.9 us
    pallas_call x1, Pallas kernels, call(): pl.pallas_call(kernel, out_shape=[jax.ShapeDtypeStruct(s, jnp.float32) fo...  24.7 us
    pallas_call x1, Pallas kernels, core_exchange(): pl.pallas_call(functools.partial(core_kernel, n_in), out_shape=jax.ShapeD...  16.7 us
    unnamed x5, local copies, waits for them, and re-layouts  4.21 us

profile of v2, /device:TPU:0, one launch (start us, length us, event | category | flops | bytes accessed | tf_op | source)
XLA Modules:
  0.0 84.1 jit_solution(11645444637089875504)
XLA Ops:
  0.6 0.0 copy-start
  0.6 1.6 %copy-done = f32[512,4,256]{2,1,0:T(4,128)S(1)} copy-done((f32[512,4,256]{2,1,0:T(4,128)S(1)}, f32[512,4,256]{2,1,0:T(4,128)}, u32[]{:S(2)}) %copy-start) | copy-done | bytes 2097176
  2.2 0.0 copy-start.1
  2.2 1.0 %copy-done.1 = f32[512,256]{1,0:T(8,128)S(1)} copy-done((f32[512,256]{1,0:T(8,128)S(1)}, f32[512,256]{1,0:T(8,128)}, u32[]{:S(2)}) %copy-start.1) | copy-done | bytes 524312
  3.3 37.9 %shard_map.41 = (f32[512,512]{1,0:T(8,128)S(1)}, f32[256,512]{1,0:T(8,128)S(1)}) custom-call(f32[512,4,256]{2,1,0:T(4,128)S(1)} %copy-done, f32[512,256]{1,0:T(8,128)S(1)} %copy-done.1), custom_call_target="tpu_custom_call" | custom-call | tf_op jit(solution)/shard_map/pallas_call | solution.py:323
  41.1 24.7 %shard_map.42 = (f32[256,512]{1,0:T(8,128)S(1)}, f32[512,256]{1,0:T(8,128)}) custom-call(f32[512,512]{1,0:T(8,128)S(1)} %get-tuple-element.6.gram_ref, f32[256,512]{1,0:T(8,128)S(1)} %get-tuple-element.7.basis_ref), custom_call_target="tpu_custom_call" | custom-call | flops 2000000000 | bytes 4194304 | tf_op jit(solution)/shard_map/pallas_call | solution.py:134
  65.8 16.7 %shard_map.43 = f32[32,32,256]{2,1,0:T(8,128)S(1)} custom-call(f32[256,512]{1,0:T(8,128)S(1)} %get-tuple-element.9.basis_ref, f32[512,4,256]{2,1,0:T(4,128)S(1)} %copy-done), custom_call_target="tpu_custom_call" | custom-call | tf_op jit(solution)/shard_map/pallas_call | solution.py:400
  82.5 1.6 %copy.4 = f32[32,32,256]{2,1,0:T(8,128)} copy(f32[32,32,256]{2,0,1:T(8,128)S(1)} %bitcast.1) | data formatting | bytes 2097152
Async XLA Ops:
  0.6 1.6 %copy-start = (f32[512,4,256]{2,1,0:T(4,128)S(1)}, f32[512,4,256]{2,1,0:T(4,128)}, u32[]{:S(2)}) copy-start(f32[512,4,256]{2,1,0:T(4,128)} %field_ref.3) | copy-start | bytes 6291460
  2.2 1.0 %copy-start.1 = (f32[512,256]{1,0:T(8,128)S(1)}, f32[512,256]{1,0:T(8,128)}, u32[]{:S(2)}) copy-start(f32[512,256]{1,0:T(8,128)} %start_ref.1) | copy-start | bytes 1572868

commit v3 on v1

v3 whole, which is shorter than its diff:
```python
import functools

import jax
import jax.numpy as jnp
from jax import lax
from jax.experimental import pallas as pl
from jax.experimental.pallas import tpu as pltpu
from jax.sharding import PartitionSpec as P

ITERS = 2
SUB = 8
LANES = 128
HIGHEST = lax.Precision.HIGHEST
HIGH = lax.Precision.HIGH


def dot(a, b, dims, precision=HIGHEST):
    return lax.dot_general(
        a, b, ((dims[0], dims[1]), ((), ())), precision=precision,
        preferred_element_type=jnp.float32,
    )


def row(x, i):
    return jnp.broadcast_to(x[i : i + 1, :], (SUB, LANES))


def factor_block(mat, inv, at):
    rows = lax.broadcasted_iota(jnp.int32, (SUB, LANES), 0)
    lanes = lax.broadcasted_iota(jnp.int32, (SUB, LANES), 1)
    groups = LANES // SUB
    a = [mat[at + g * SUB : at + (g + 1) * SUB, at : at + LANES] for g in range(groups)]
    x = [jnp.where(rows + g * SUB == lanes, 1.0, 0.0).astype(jnp.float32) for g in range(groups)]
    for s in range(groups):
        later = range(s + 1, groups)
        wide = [
            {
                g: jnp.broadcast_to(a[g][:, s * SUB + k : s * SUB + k + 1], (SUB, LANES))
                for g in range(s, groups)
            }
            for k in range(SUB)
        ]
        splat = [[row(wide[k][s], i) for i in range(k, SUB)] for k in range(SUB)]
        root, low = [], []
        for j in range(SUB):
            root.append(lax.rsqrt(splat[j][0]))
            low.append([v * root[j] for v in splat[j][1:]])
            for k in range(j + 1, SUB):
                by = low[j][k - j - 1]
                splat[k] = [v - low[j][k - j - 1 + i] * by for i, v in enumerate(splat[k])]
        scale = jnp.zeros((SUB, LANES), jnp.float32)
        upper_a, upper_x = [], []
        for j in range(SUB):
            scale = jnp.where(rows == j, root[j], scale)
            upper_a.append(row(a[s], j) * root[j])
            upper_x.append(row(x[s], j) * root[j])
            if j < SUB - 1:
                column = jnp.zeros((SUB, LANES), jnp.float32)
                for i in range(j + 1, SUB):
                    column = jnp.where(rows == i, low[j][i - j - 1], column)
                a[s] = a[s] - column * upper_a[j]
                x[s] = x[s] - column * upper_x[j]
        x[s] = x[s] * scale
        inv[at + s * SUB : at + (s + 1) * SUB, :] = x[s]
        for g in later:
            for j in range(SUB):
                column = wide[j][g] * root[j]
                for k in range(j + 1, SUB):
                    wide[k][g] = wide[k][g] - column * low[j][k - j - 1]
                a[g] = a[g] - column * upper_a[j]
                x[g] = x[g] - column * upper_x[j]
        yield


def orthonormal(block, mat, inv):
    rank = block.shape[0]
    mat[...] = dot(block[...], block[...], ((1,), (1,)))
    for at in range(0, rank, LANES):
        yield from factor_block(mat, inv, at)
        here, below = slice(at, at + LANES), range(at + LANES, rank, LANES)
        upper = [
            dot(inv[here, :], mat[here, c : c + LANES], ((1,), (0,))) for c in below
        ]
        for i, c in enumerate(below):
            for j, d in enumerate(below):
                if d >= c:
                    mat[c : c + LANES, d : d + LANES] -= dot(upper[i], upper[j], ((0,), (0,)))
        done = dot(inv[here, :], block[here, :], ((1,), (0,)))
        block[here, :] = done
        for i, c in enumerate(below):
            block[c : c + LANES, :] -= dot(upper[i], done, ((0,), (0,)))


def sweeps_kernel(gram_ref, basis_ref, out_ref, factor_ref, mat, inv):
    out_ref[...] = basis_ref[...]

    def sweep(_, carry):
        out_ref[...] = dot(out_ref[...], gram_ref[...], ((1,), (0,)))
        for _ in orthonormal(out_ref, mat, inv):
            pass
        return carry

    lax.fori_loop(0, ITERS, sweep, 0)
    factor_ref[...] = out_ref[...].T


def call(kernel, outs, rank, *args):
    return pl.pallas_call(
        kernel,
        out_shape=[jax.ShapeDtypeStruct(s, jnp.float32) for s in outs],
        in_specs=[pl.BlockSpec(memory_space=pltpu.VMEM)] * len(args),
        out_specs=[pl.BlockSpec(memory_space=pltpu.VMEM)] * len(outs),
        scratch_shapes=[
            pltpu.VMEM((rank, rank), jnp.float32), pltpu.VMEM((rank, LANES), jnp.float32)
        ],
        compiler_params=pltpu.CompilerParams(vmem_limit_bytes=32 * 2**20),
        cost_estimate=pl.CostEstimate(
            flops=2 * 10**9, bytes_accessed=4 * 2**20, transcendentals=0
        ),
    )(*args)


MESH = pl.DeviceIdType.MESH


def upper_blocks(order):
    count = order // LANES
    return [(i, j) for i in range(count) for j in range(i, count)]


def peers(n_out, n_in):
    out, inn = lax.axis_index("outer"), lax.axis_index("inner")
    core, chip, chips = lax.rem(inn, 2), inn // 2, n_in // 2
    twin = (out, inn + 1 - 2 * core)
    plane = [
        (lax.rem(chip + d, chips), lax.rem(chip + chips - d, chips)) for d in range(1, chips)
    ]
    line = [(lax.rem(out + d, n_out), lax.rem(out + n_out - d, n_out)) for d in range(1, n_out)]
    return out, core, chip, twin, plane, line


def rows_at(start, size):
    return pl.ds(pl.multiple_of(start, 8), size)


def remote(src, dst, sems, at, device):
    return pltpu.make_async_remote_copy(
        src_ref=src, dst_ref=dst, send_sem=sems[0].at[at], recv_sem=sems[1].at[at],
        device_id=device, device_id_type=MESH,
    )


def gram_kernel(
    n_out, n_in, unfolded, start_ref, gram_ref, basis_ref, part, total, got_core, got_chip,
    got_out, mat, inv, send_sem, recv_sem,
):
    order = unfolded.shape[0]
    out, core, chip, twin, plane, line = peers(n_out, n_in)
    chips = n_in // 2
    sems = (send_sem, recv_sem)
    barrier = pltpu.get_barrier_semaphore()
    pl.semaphore_signal(barrier, inc=1, device_id=twin, device_id_type=MESH)
    for to, _ in plane:
        pl.semaphore_signal(barrier, inc=1, device_id=(out, to * 2 + core), device_id_type=MESH)
    for to, _ in line:
        pl.semaphore_signal(
            barrier, inc=1, device_id=(to, chip * 2 + core), device_id_type=MESH
        )

    places = {pair: at for at, pair in enumerate(upper_blocks(order))}
    size = len(places) * LANES
    if part.shape[0] > size:
        part[size:, :] = jnp.zeros((part.shape[0] - size, LANES), jnp.float32)
    wide = 2 * LANES
    for i in range(0, order, wide):
        for j in range(i, order, wide):
            block = dot(
                unfolded[i : i + wide, :], unfolded[j : j + wide, :], ((1,), (1,)), HIGH
            )
            for a in range(2):
                for b in range(2):
                    pair = (i // LANES + a, j // LANES + b)
                    if pair in places:
                        at = places[pair] * LANES
                        part[at : at + LANES, :] = block[
                            a * LANES : (a + 1) * LANES, b * LANES : (b + 1) * LANES
                        ]

    basis_ref[...] = start_ref[...].T
    blocks = orthonormal(basis_ref, mat, inv)
    count = mat.shape[0] // SUB + 1

    def run(steps):
        for _ in range(steps):
            next(blocks, None)

    pl.semaphore_wait(barrier, 1 + len(plane) + len(line))

    half = part.shape[0] // 2
    quarter = half // chips
    piece = quarter // n_out
    mine = core * half
    copy = remote(part.at[rows_at((1 - core) * half, half)], got_core, sems, 0, twin)
    copy.start()
    run(11)
    copy.wait()
    part[rows_at(mine, half), :] += got_core[...]

    copies = []
    for d, (to, _) in enumerate(plane):
        copies.append(
            remote(
                part.at[rows_at(mine + to * quarter, quarter)], got_chip.at[d], sems, 1 + d,
                (out, to * 2 + core),
            )
        )
        copies[-1].start()
    run(11)
    for copy in copies:
        copy.wait()
    mine = mine + chip * quarter
    value = part[rows_at(mine, quarter), :]
    for d in range(len(plane)):
        value += got_chip[d]
    part[rows_at(mine, quarter), :] = value

    base = 1 + len(plane)
    copies = []
    for d, (to, _) in enumerate(line):
        copies.append(
            remote(
                part.at[rows_at(mine + to * piece, piece)], got_out.at[d], sems, base + d,
                (to, chip * 2 + core),
            )
        )
        copies[-1].start()
    run(7)
    for copy in copies:
        copy.wait()
    own = mine + out * piece
    value = part[rows_at(own, piece), :]
    for d in range(len(line)):
        value += got_out[d]
    total[rows_at(own, piece), :] = value

    base += len(line)
    copies = []
    for d, (to, _) in enumerate(line):
        spot = total.at[rows_at(own, piece)]
        copies.append(remote(spot, spot, sems, base + d, (to, chip * 2 + core)))
        copies[-1].start()
    run(7)
    for copy in copies:
        copy.wait()
    base += len(line)
    copies = []
    for d, (to, _) in enumerate(plane):
        spot = total.at[rows_at(mine, quarter)]
        copies.append(remote(spot, spot, sems, base + d, (out, to * 2 + core)))
        copies[-1].start()
    run(9)
    base += len(plane)
    forwards = []
    for d in range(1 + len(plane)):
        if d:
            copies[d - 1].wait_recv()
        origin = plane[d - 1][1] if d else chip
        spot = total.at[rows_at(core * half + origin * quarter, quarter)]
        forwards.append(remote(spot, spot, sems, base + d, twin))
        forwards[-1].start()
    run(count)
    for copy in copies:
        copy.wait_send()
    for copy in forwards:
        copy.wait()

    for (i, j), at in places.items():
        block = total[at * LANES : (at + 1) * LANES, :]
        gram_ref[i * LANES : (i + 1) * LANES, j * LANES : (j + 1) * LANES] = block
        if i != j:
            gram_ref[j * LANES : (j + 1) * LANES, i * LANES : (i + 1) * LANES] = block.T


def gram_sum(mesh, unfolded, start_block):
    rank = start_block.shape[1]
    n_out, n_in = mesh.shape["outer"], mesh.shape["inner"]
    order = unfolded.shape[0]
    chips = n_in // 2
    unit = 8 * n_out * n_in
    rows = -(-len(upper_blocks(order)) * LANES // unit) * unit
    half = rows // 2
    sems = 2 + 3 * (chips - 1) + 2 * (n_out - 1)
    f32 = jnp.float32
    return pl.pallas_call(
        functools.partial(gram_kernel, n_out, n_in),
        out_shape=[
            jax.ShapeDtypeStruct((order, order), f32),
            jax.ShapeDtypeStruct((rank, order), f32),
        ],
        in_specs=[pl.BlockSpec(memory_space=pltpu.VMEM)] * 2,
        out_specs=[pl.BlockSpec(memory_space=pltpu.VMEM)] * 2,
        scratch_shapes=[
            pltpu.VMEM((rows, LANES), f32),
            pltpu.VMEM((rows, LANES), f32),
            pltpu.VMEM((half, LANES), f32),
            pltpu.VMEM((max(chips - 1, 1), half // chips, LANES), f32),
            pltpu.VMEM((max(n_out - 1, 1), half // chips // n_out, LANES), f32),
            pltpu.VMEM((rank, rank), f32),
            pltpu.VMEM((rank, LANES), f32),
            pltpu.SemaphoreType.DMA((sems,)),
            pltpu.SemaphoreType.DMA((sems,)),
        ],
        compiler_params=pltpu.CompilerParams(
            collective_id=0, has_side_effects=True, vmem_limit_bytes=40 * 2**20
        ),
    )(unfolded, start_block)


def core_kernel(n_in, basis_ref, unfolded, fibres_ref, core, load_sem, send_sem, recv_sem):
    second, _, third = core.shape
    rank = basis_ref.shape[0]
    share = rank // n_in
    out, inn = lax.axis_index("outer"), lax.axis_index("inner")
    barrier = pltpu.get_barrier_semaphore()
    targets = [lax.rem(inn + d, n_in) for d in range(1, n_in)]
    for to in targets:
        pl.semaphore_signal(barrier, inc=1, device_id=(out, to), device_id_type=MESH)
    copies = []
    for i in range(second):
        core[i] = dot(
            basis_ref[...], unfolded[:, i * third : (i + 1) * third], ((1,), (0,)), HIGH
        )
        if i == 0:
            pl.semaphore_wait(barrier, n_in - 1)
        for d, to in enumerate(targets):
            copies.append(
                pltpu.make_async_remote_copy(
                    src_ref=core.at[i, rows_at(to * share, share)],
                    dst_ref=fibres_ref.at[inn * second + i],
                    send_sem=send_sem.at[i, d],
                    recv_sem=recv_sem.at[i, d],
                    device_id=(out, to),
                    device_id_type=MESH,
                )
            )
            copies[-1].start()
        copies.append(
            pltpu.make_async_copy(
                core.at[i, rows_at(inn * share, share)],
                fibres_ref.at[inn * second + i],
                load_sem.at[i],
            )
        )
        copies[-1].start()
    for copy in copies:
        copy.wait()


def core_exchange(mesh, basis, unfolded, second):
    n_in = mesh.shape["inner"]
    third = unfolded.shape[1] // second
    rank = basis.shape[0]
    f32 = jnp.float32
    return pl.pallas_call(
        functools.partial(core_kernel, n_in),
        out_shape=jax.ShapeDtypeStruct((n_in * second, rank // n_in, third), f32),
        in_specs=[pl.BlockSpec(memory_space=pltpu.VMEM)] * 2,
        out_specs=pl.BlockSpec(memory_space=pl.ANY),
        scratch_shapes=[
            pltpu.VMEM((second, rank, third), f32),
            pltpu.SemaphoreType.DMA((second,)),
            pltpu.SemaphoreType.DMA((second, n_in - 1)),
            pltpu.SemaphoreType.DMA((second, n_in - 1)),
        ],
        compiler_params=pltpu.CompilerParams(
            collective_id=1, has_side_effects=True, vmem_limit_bytes=40 * 2**20
        ),
    )(basis, unfolded)


def on_device(mesh, field_slab, start_block):
    order, second, third = field_slab.shape
    unfolded = field_slab.reshape(order, second * third)
    rank = start_block.shape[1]
    gram_total, basis = gram_sum(mesh, unfolded, start_block)
    basis, factor = call(
        sweeps_kernel, [(rank, order), (order, rank)], rank, gram_total, basis
    )
    fibres = core_exchange(mesh, basis, unfolded, second)
    return (factor, fibres.transpose(1, 0, 2))


def solution(mesh):
    return jax.shard_map(
        functools.partial(on_device, mesh),
        mesh=mesh,
        in_specs=(P(None, "inner", "outer"), P()),
        out_specs=(P(), P("inner", None, "outer")),
        check_vma=False,
    )
```

time: 84.7 us -> 76.1 us (0.90)
  Pallas kernels: 81.1 us -> 71.5 us
  local copies, waits for them, and re-layouts: 2.77 us -> 3.7 us
    pallas_call x2 -> x1, Pallas kernels: 36 us -> 24.4 us  [call(): pl.pallas_call(kernel, out_shape=[jax.ShapeDtypeStruct(s, jnp.float32) fo...]
    pallas_call x1, Pallas kernels: 28.4 us -> 32 us  [gram_sum(): pl.pallas_call(functools.partial(gram_kernel, n_out, n_in), out_shape=[ja...]
    pallas_call x1, Pallas kernels: 16.7 us -> 15.1 us  [core_exchange(): pl.pallas_call(functools.partial(core_kernel, n_in), out_shape=jax.ShapeD...]
    unnamed x5 -> x4, local copies, waits for them, and re-layouts: 2.77 us -> 3.7 us
where the time goes in v3:
time: 76.1 us; the launch traced here: 75.9 us
  Pallas kernels  71.5 us (94%)
  local copies, waits for them, and re-layouts  3.7 us (5%)
    pallas_call x1, Pallas kernels, gram_sum(): pl.pallas_call(functools.partial(gram_kernel, n_out, n_in), out_shape=[ja...  32 us
    pallas_call x1, Pallas kernels, call(): pl.pallas_call(kernel, out_shape=[jax.ShapeDtypeStruct(s, jnp.float32) fo...  24.4 us
    pallas_call x1, Pallas kernels, core_exchange(): pl.pallas_call(functools.partial(core_kernel, n_in), out_shape=jax.ShapeD...  15.1 us
    unnamed x4, local copies, waits for them, and re-layouts  3.7 us

profile of v3, /device:TPU:0, one launch (start us, length us, event | category | flops | bytes accessed | tf_op | source)
XLA Modules:
  0.0 75.9 jit_solution(4183386209807693753)
XLA Ops:
  0.6 0.0 copy-start
  0.6 2.1 %copy.5 = f32[64,8,4,256]{3,1,2,0:T(8,128)S(1)} copy(f32[64,8,4,256]{3,2,1,0:T(4,128)} %bitcast.6) | data formatting | bytes 4194304
  2.8 0.0 copy-done
  2.8 32.0 %shard_map.41 = (f32[512,512]{1,0:T(8,128)S(1)}, f32[256,512]{1,0:T(8,128)S(1)}) custom-call(f32[512,1024]{1,0:T(8,128)S(1)} %bitcast.3, f32[512,256]{1,0:T(8,128)S(1)} %copy-done), custom_call_target="tpu_custom_call" | custom-call | tf_op jit(solution)/shard_map/pallas_call | solution.py:294
  34.8 24.4 %shard_map.42 = (f32[256,512]{1,0:T(8,128)S(1)}, f32[512,256]{1,0:T(8,128)}) custom-call(f32[512,512]{1,0:T(8,128)S(1)} %get-tuple-element.6.gram_ref, f32[256,512]{1,0:T(8,128)S(1)} %get-tuple-element.7.basis_ref), custom_call_target="tpu_custom_call" | custom-call | flops 2000000000 | bytes 4194304 | tf_op jit(solution)/shard_map/pallas_call | solution.py:108
  59.2 15.1 %shard_map.43 = f32[32,32,256]{2,1,0:T(8,128)S(1)} custom-call(f32[256,512]{1,0:T(8,128)S(1)} %get-tuple-element.9.basis_ref, f32[512,1024]{1,0:T(8,128)S(1)} %bitcast.4), custom_call_target="tpu_custom_call" | custom-call | tf_op jit(solution)/shard_map/pallas_call | solution.py:364
  74.3 1.6 %copy.4 = f32[32,32,256]{2,1,0:T(8,128)} copy(f32[32,32,256]{2,0,1:T(8,128)S(1)} %bitcast.5) | data formatting | bytes 2097152
Async XLA Ops:
  0.6 2.1 %copy-start = (f32[512,256]{1,0:T(8,128)S(1)}, f32[512,256]{1,0:T(8,128)}, u32[]{:S(2)}) copy-start(f32[512,256]{1,0:T(8,128)} %start_ref.1) | copy-start | bytes 1572868

commit v4 on v3

--- a/solution.py
+++ b/solution.py
@@ -74,7 +74,8 @@
 
 def orthonormal(block, mat, inv):
     rank = block.shape[0]
-    mat[...] = dot(block[...], block[...], ((1,), (1,)))
+    for at in range(0, rank, LANES):
+        mat[at : at + LANES, at:] = dot(block[at : at + LANES, :], block[at:, :], ((1,), (1,)))
     for at in range(0, rank, LANES):
         yield from factor_block(mat, inv, at)
         here, below = slice(at, at + LANES), range(at + LANES, rank, LANES)
@@ -95,7 +96,7 @@
     out_ref[...] = basis_ref[...]
 
     def sweep(_, carry):
-        out_ref[...] = dot(out_ref[...], gram_ref[...], ((1,), (0,)))
+        out_ref[...] = dot(out_ref[...], gram_ref[...], ((1,), (0,)), HIGH)
         for _ in orthonormal(out_ref, mat, inv):
             pass
         return carry
@@ -172,11 +173,18 @@
     if part.shape[0] > size:
         part[size:, :] = jnp.zeros((part.shape[0] - size, LANES), jnp.float32)
     wide = 2 * LANES
+    whole = unfolded[...]
+    high = whole.astype(jnp.bfloat16)
+    rest = (whole - high.astype(jnp.float32)).astype(jnp.bfloat16)
+
+    def times(first, second, i, j):
+        return dot(first[i : i + wide, :], second[j : j + wide, :], ((1,), (1,)), None)
+
     for i in range(0, order, wide):
         for j in range(i, order, wide):
-            block = dot(
-                unfolded[i : i + wide, :], unfolded[j : j + wide, :], ((1,), (1,)), HIGH
-            )
+            cross = times(high, rest, i, j)
+            cross += cross.T if i == j else times(rest, high, i, j)
+            block = times(high, high, i, j) + cross
             for a in range(2):
                 for b in range(2):
                     pair = (i // LANES + a, j // LANES + b)

time: 76.1 us -> 74.9 us (0.984)
  Pallas kernels: 71.5 us -> 70.4 us
where the time goes in v4:
time: 74.9 us; the launch traced here: 74.8 us
  Pallas kernels  70.4 us (94%)
  local copies, waits for them, and re-layouts  3.7 us (5%)
    pallas_call x1, Pallas kernels, gram_sum(): pl.pallas_call(functools.partial(gram_kernel, n_out, n_in), out_shape=[ja...  31.5 us
    pallas_call x1, Pallas kernels, call(): pl.pallas_call(kernel, out_shape=[jax.ShapeDtypeStruct(s, jnp.float32) fo...  23.9 us
    pallas_call x1, Pallas kernels, core_exchange(): pl.pallas_call(functools.partial(core_kernel, n_in), out_shape=jax.ShapeD...  15 us
    unnamed x4, local copies, waits for them, and re-layouts  3.7 us

profile of v4, /device:TPU:0, one launch (start us, length us, event | category | flops | bytes accessed | tf_op | source)
XLA Modules:
  0.0 74.8 jit_solution(16356876669402384318)
XLA Ops:
  0.6 0.0 copy-start
  0.6 2.1 %copy.5 = f32[64,8,4,256]{3,1,2,0:T(8,128)S(1)} copy(f32[64,8,4,256]{3,2,1,0:T(4,128)} %bitcast.6) | data formatting | bytes 4194304
  2.8 0.0 copy-done
  2.8 31.5 %shard_map.41 = (f32[512,512]{1,0:T(8,128)S(1)}, f32[256,512]{1,0:T(8,128)S(1)}) custom-call(f32[512,1024]{1,0:T(8,128)S(1)} %bitcast.3, f32[512,256]{1,0:T(8,128)S(1)} %copy-done), custom_call_target="tpu_custom_call" | custom-call | tf_op jit(solution)/shard_map/pallas_call | solution.py:302
  34.3 23.9 %shard_map.42 = (f32[256,512]{1,0:T(8,128)S(1)}, f32[512,256]{1,0:T(8,128)}) custom-call(f32[512,512]{1,0:T(8,128)S(1)} %get-tuple-element.6.gram_ref, f32[256,512]{1,0:T(8,128)S(1)} %get-tuple-element.7.basis_ref), custom_call_target="tpu_custom_call" | custom-call | flops 2000000000 | bytes 4194304 | tf_op jit(solution)/shard_map/pallas_call | solution.py:109
  58.1 15.0 %shard_map.43 = f32[32,32,256]{2,1,0:T(8,128)S(1)} custom-call(f32[256,512]{1,0:T(8,128)S(1)} %get-tuple-element.9.basis_ref, f32[512,1024]{1,0:T(8,128)S(1)} %bitcast.4), custom_call_target="tpu_custom_call" | custom-call | tf_op jit(solution)/shard_map/pallas_call | solution.py:372
  73.2 1.6 %copy.4 = f32[32,32,256]{2,1,0:T(8,128)} copy(f32[32,32,256]{2,0,1:T(8,128)S(1)} %bitcast.5) | data formatting | bytes 2097152
Async XLA Ops:
  0.6 2.1 %copy-start = (f32[512,256]{1,0:T(8,128)S(1)}, f32[512,256]{1,0:T(8,128)}, u32[]{:S(2)}) copy-start(f32[512,256]{1,0:T(8,128)} %start_ref.1) | copy-start | bytes 1572868
